TPU v7x, 32 devices: a whole 2x2x4 slice. The times are simulated.
32 devices in a mesh: seq: 16 (over z, y, x), head: 2 (over core).
Axes of the slice: x: 2, y: 2, z: 4, core: 2. Of those that a mesh axis runs over, the one named last changes fastest.
Arguments:
- queries: bfloat16 [16384, 1024], P('seq', 'head'), may hold values from -14 to 14
- key_rows: bfloat16 [16384, 1024], P('seq', 'head'), may hold values from -14 to 14
- value_rows: bfloat16 [16384, 1024], P('seq', 'head'), may hold values from -8 to 8
- out_weight: bfloat16 [1024, 1024], P('head'), may hold values from -0.1875 to 0.1875
Outputs:
- mixed: bfloat16 [16384, 1024], P('seq', 'head')
All inputs are finite; a program needn't handle non-finite values.
Results may differ from a plain program's by a relative error of at most 0.012.
Values may be sent and summed in bfloat16 or wider, within the bound.
A program may use at most 128 MiB of HBM per device.

v0:
```python
import jax
import jax.numpy as jnp
from jax import lax
from jax.sharding import PartitionSpec as P

HEAD_DIM = 64
BLOCK = 256
LEVELS = 6
LOCAL_LEVELS = 3


LOG_TWO = 0.6931471805599453
NEG_LARGE = -1e30


def shifted(value, axis, steps):
    count = lax.axis_size(axis)
    leading, last = (max(0, -steps), min(count, count - steps))
    return lax.ppermute(value, axis, [(source, source + steps) for source in range(leading, last)])


def padded_2(cells, sides, width):
    for axis, dim in sides:
        count = lax.axis_size(axis)
        ends = count - 1
        head = lax.slice_in_dim(cells, 0, width, axis=dim)
        tail = lax.slice_in_dim(cells, cells.shape[dim] - width, cells.shape[dim], axis=dim)
        cells = jnp.concatenate(
            [
                lax.ppermute(tail, axis, [(i, (i + 1) % count) for i in range(ends)]),
                cells,
                lax.ppermute(head, axis, [((i + 1) % count, i) for i in range(ends)]),
            ],
            axis=dim,
        )
    return cells


def coarsen(rows_in):
    row_count = rows_in.shape[-2]
    widened = rows_in.astype(jnp.float32).reshape(
        rows_in.shape[:-2] + (row_count // 2, 2, rows_in.shape[-1])
    )
    return ((widened[..., 0, :] + widened[..., 1, :]) * 0.5).astype(jnp.bfloat16)


def attend_groups(query_part, key_part, value_part, valid_keys, height):
    scores = jnp.einsum("gqhd,gkhd->ghqk", query_part, key_part, preferred_element_type=jnp.float32)
    scores = scores * HEAD_DIM ** (-0.5) + height * LOG_TWO
    scores = jnp.where(valid_keys[:, None, None, :], scores, NEG_LARGE)
    row_peak = jnp.max(scores, axis=-1)
    weights = jnp.exp(scores - row_peak[..., None])
    row_total = jnp.sum(weights, axis=-1)
    numerator = jnp.einsum(
        "ghqk,gkhd->gqhd",
        weights.astype(jnp.bfloat16),
        value_part,
        preferred_element_type=jnp.float32,
    )
    return (jnp.swapaxes(row_peak, 1, 2), jnp.swapaxes(row_total, 1, 2), numerator)


def local_level(query_level, padded, height, first_block, all_blocks):
    row_count, columns = query_level.shape
    heads_here = columns // HEAD_DIM
    blocks = row_count // BLOCK
    key_blocks = padded[0].reshape(blocks + 2, BLOCK, heads_here, HEAD_DIM)
    value_blocks = padded[1].reshape(blocks + 2, BLOCK, heads_here, HEAD_DIM)
    offsets = [0, 1, 2] if height == 0 else [0, 2]
    keys_all = jnp.concatenate([key_blocks[offset : offset + blocks] for offset in offsets], axis=1)
    values_all = jnp.concatenate(
        [value_blocks[offset : offset + blocks] for offset in offsets], axis=1
    )
    block_ids = first_block + jnp.arange(blocks, dtype=jnp.int32)
    block_flags = [
        (block_ids + offset - 1 >= 0) & (block_ids + offset - 1 < all_blocks) for offset in offsets
    ]
    valid_keys = jnp.concatenate(
        [jnp.repeat(flag_row[:, None], BLOCK, axis=1) for flag_row in block_flags], axis=1
    )
    per_step = 2 if blocks % 2 == 0 else 1
    step_count = blocks // per_step
    key_count = keys_all.shape[1]

    def one_step(pieces):
        query_part, key_part, value_part, valid_part = pieces
        return attend_groups(query_part, key_part, value_part, valid_part, height)

    row_peak, row_total, numerator = lax.map(
        one_step,
        (
            query_level.reshape(step_count, per_step, BLOCK, heads_here, HEAD_DIM),
            keys_all.reshape(step_count, per_step, key_count, heads_here, HEAD_DIM),
            values_all.reshape(step_count, per_step, key_count, heads_here, HEAD_DIM),
            valid_keys.reshape(step_count, per_step, key_count),
        ),
    )
    return (
        row_peak.reshape(row_count, heads_here),
        row_total.reshape(row_count, heads_here),
        numerator.reshape(row_count, heads_here, HEAD_DIM),
    )


def upper_level(query_level, pair_rows, height, seq_index, base_row, length):
    row_count, columns = query_level.shape
    heads_here = columns // HEAD_DIM
    all_blocks = length // BLOCK
    block_id = seq_index * row_count // BLOCK
    left_start = jnp.clip((block_id - 1) * BLOCK, 0, length - BLOCK) - base_row
    right_start = jnp.clip((block_id + 1) * BLOCK, 0, length - BLOCK) - base_row
    left_part = lax.dynamic_slice_in_dim(pair_rows, left_start, BLOCK, axis=1)
    right_part = lax.dynamic_slice_in_dim(pair_rows, right_start, BLOCK, axis=1)
    joined = jnp.concatenate([left_part, right_part], axis=1)
    block_flags = jnp.stack([block_id >= 1, block_id + 1 < all_blocks])
    valid_keys = jnp.repeat(block_flags, BLOCK)[None, :]
    row_peak, row_total, numerator = attend_groups(
        query_level.reshape(1, row_count, heads_here, HEAD_DIM),
        joined[0].reshape(1, 2 * BLOCK, heads_here, HEAD_DIM),
        joined[1].reshape(1, 2 * BLOCK, heads_here, HEAD_DIM),
        valid_keys,
        height,
    )
    return (row_peak[0], row_total[0], numerator[0])


def window_near(rows_in, span):
    distances = list(range(span, 0, -1)) + list(range(-1, -span - 1, -1))
    moved = [shifted(rows_in, "seq", distance) for distance in distances]
    return jnp.concatenate(moved[:span] + [rows_in] + moved[span:], axis=1)


def local(queries, key_rows, value_rows, out_weight):
    tok_rows, columns = queries.shape
    seq_count = lax.axis_size("seq")
    seq_index = lax.axis_index("seq")
    query_levels = [queries]
    pair_levels = [jnp.stack([key_rows, value_rows])]
    for height in range(1, LEVELS):
        query_levels.append(coarsen(query_levels[-1]))
        pair_levels.append(coarsen(pair_levels[-1]))
    results = []
    for height in range(LOCAL_LEVELS):
        padded = padded_2(pair_levels[height], (("seq", 1),), BLOCK)
        blocks = (tok_rows >> height) // BLOCK
        results.append(
            local_level(
                query_levels[height], padded, height, seq_index * blocks, seq_count * blocks
            )
        )
    level_rows = pair_levels[LOCAL_LEVELS].shape[1]
    span = 2 ** (LEVELS - LOCAL_LEVELS + 1) - 1
    reach = level_rows * span
    window = window_near(pair_levels[LOCAL_LEVELS], span)
    for height in range(LOCAL_LEVELS, LEVELS):
        if height > LOCAL_LEVELS:
            window = coarsen(window)
            reach = reach // 2
        row_count = query_levels[height].shape[0]
        results.append(
            upper_level(
                query_levels[height],
                window,
                height,
                seq_index,
                seq_index * row_count - reach,
                seq_count * row_count,
            )
        )
    run_peak, run_total, run_numer = results[0]
    for height in range(1, LEVELS):
        row_peak, row_total, numerator = results[height]
        factor = 2**height
        row_peak = jnp.repeat(row_peak, factor, axis=0)
        row_total = jnp.repeat(row_total, factor, axis=0)
        numerator = jnp.repeat(numerator, factor, axis=0)
        newest = jnp.maximum(run_peak, row_peak)
        keep_scale = jnp.exp(run_peak - newest)
        fresh_scale = jnp.exp(row_peak - newest)
        run_total = run_total * keep_scale + row_total * fresh_scale
        run_numer = run_numer * keep_scale[..., None] + numerator * fresh_scale[..., None]
        run_peak = newest
    attended = (run_numer / run_total[..., None]).astype(jnp.bfloat16).reshape(tok_rows, columns)
    partial_term = jnp.dot(attended, out_weight, preferred_element_type=jnp.float32)
    return lax.psum_scatter(
        partial_term.astype(jnp.bfloat16), "head", scatter_dimension=1, tiled=True
    )


def solution(mesh):
    return jax.shard_map(
        local,
        mesh=mesh,
        in_specs=(P("seq", "head"), P("seq", "head"), P("seq", "head"), P("head", None)),
        out_specs=P("seq", "head"),
        check_vma=False,
    )
```

profile of v0, /device:TPU:29, one launch (start us, length us, event | category | flops | bytes accessed | tf_op | source)
XLA Modules:
  0.0 577.1 jit_solution(11444615936063024363)
XLA Ops:
  25.5 3.8 fusion.125
  33.7 2.9 reshape.729
  39.2 2.9 reshape.730
  64.8 3.9 reshape.738
  74.5 3.0 copy.257
  85.5 5.9 %collective-permute-done.9 = bf16[2,128,512]{2,0,1:T(2,128)(2,1)S(1)} collective-permute-done((bf16[2,128,512]{2,0,1:T(2,128)(2,1)}, bf16[2,128,512]{2,0,1:T(2,128)(2,1)S(1)}, u32[]{:S(2)}, u32[]{:S(2)}) %collective-permute-start.9) | collective-permute-done | bytes 262176 | tf_op jit(solution)/shard_map/ppermute | solution.py:19
  92.9 3.3 collective-permute-done.10
  97.9 29.2 %collective-permute-done.11 = bf16[2,128,512]{2,0,1:T(2,128)(2,1)S(1)} collective-permute-done((bf16[2,128,512]{2,0,1:T(2,128)(2,1)}, bf16[2,128,512]{2,0,1:T(2,128)(2,1)S(1)}, u32[]{:S(2)}, u32[]{:S(2)}) %collective-permute-start.11) | collective-permute-done | bytes 262176 | tf_op jit(solution)/shard_map/ppermute | solution.py:19
  128.6 4.2 collective-permute-done.12
  139.7 9.8 %collective-permute-done.15 = bf16[2,128,512]{2,0,1:T(2,128)(2,1)S(1)} collective-permute-done((bf16[2,128,512]{2,0,1:T(2,128)(2,1)}, bf16[2,128,512]{2,0,1:T(2,128)(2,1)S(1)}, u32[]{:S(2)}, u32[]{:S(2)}) %collective-permute-start.15) | collective-permute-done | bytes 262176 | tf_op jit(solution)/shard_map/ppermute | solution.py:19
  151.0 4.8 collective-permute-done.16
  157.4 6.1 %collective-permute-start.20 = (bf16[2,128,512]{2,0,1:T(2,128)(2,1)}, bf16[2,128,512]{2,0,1:T(2,128)(2,1)S(1)}, u32[]{:S(2)}, u32[]{:S(2)}) collective-permute-start(bf16[2,128,512]{2,0,1:T(2,128)(2,1)} %fusion.86), channel_id=1, source_target_pairs={{0,2},{2,4},{4,6},{6,8},{8,10},{10,12},{12,14},{14,16},{16,18},{18... | collective-permute-start | bytes 786440 | tf_op jit(solution)/shard_map/ppermute | solution.py:19
  163.7 3.2 collective-permute-done.18
  168.5 3.6 collective-permute-start.22
  172.8 5.0 collective-permute-start.21
  178.4 9.6 %collective-permute-done.21 = bf16[2,128,512]{2,0,1:T(2,128)(2,1)S(1)} collective-permute-done((bf16[2,128,512]{2,0,1:T(2,128)(2,1)}, bf16[2,128,512]{2,0,1:T(2,128)(2,1)S(1)}, u32[]{:S(2)}, u32[]{:S(2)}) %collective-permute-start.21) | collective-permute-done | bytes 262176 | tf_op jit(solution)/shard_map/ppermute | solution.py:19
  195.6 5.9 %collective-permute-start.27 = (bf16[2,128,512]{2,0,1:T(2,128)(2,1)}, bf16[2,128,512]{2,0,1:T(2,128)(2,1)S(1)}, u32[]{:S(2)}, u32[]{:S(2)}) collective-permute-start(bf16[2,128,512]{2,0,1:T(2,128)(2,1)} %fusion.86), channel_id=1, source_target_pairs={{14,0},{16,2},{18,4},{20,6},{22,8},{24,10},{26,12},{28,14},{30,16}... | collective-permute-start | bytes 786440 | tf_op jit(solution)/shard_map/ppermute | solution.py:19
  201.7 5.4 collective-permute-start.28
  207.3 6.3 %collective-permute-start.29 = (bf16[2,128,512]{2,0,1:T(2,128)(2,1)}, bf16[2,128,512]{2,0,1:T(2,128)(2,1)S(1)}, u32[]{:S(2)}, u32[]{:S(2)}) collective-permute-start(bf16[2,128,512]{2,0,1:T(2,128)(2,1)} %fusion.86), channel_id=1, source_target_pairs={{18,0},{20,2},{22,4},{24,6},{26,8},{28,10},{30,12},{19,1},{21,3},{... | collective-permute-start | bytes 786440 | tf_op jit(solution)/shard_map/ppermute | solution.py:19
  213.9 3.4 collective-permute-start.30
  218.1 28.9 %collective-permute-start.31 = (bf16[2,128,512]{2,0,1:T(2,128)(2,1)}, bf16[2,128,512]{2,0,1:T(2,128)(2,1)S(1)}, u32[]{:S(2)}, u32[]{:S(2)}) collective-permute-start(bf16[2,128,512]{2,0,1:T(2,128)(2,1)} %fusion.86), channel_id=1, source_target_pairs={{22,0},{24,2},{26,4},{28,6},{30,8},{23,1},{25,3},{27,5},{29,7},{31... | collective-permute-start | bytes 786440 | tf_op jit(solution)/shard_map/ppermute | solution.py:19
  247.2 5.4 collective-permute-start.32
  252.8 17.5 %collective-permute-start.33 = (bf16[2,128,512]{2,0,1:T(2,128)(2,1)}, bf16[2,128,512]{2,0,1:T(2,128)(2,1)S(1)}, u32[]{:S(2)}, u32[]{:S(2)}) collective-permute-start(bf16[2,128,512]{2,0,1:T(2,128)(2,1)} %fusion.86), channel_id=1, source_target_pairs={{26,0},{28,2},{30,4},{27,1},{29,3},{31,5}} | collective-permute-start | bytes 786440 | tf_op jit(solution)/shard_map/ppermute | solution.py:19
  272.7 4.1 collective-permute-start.4
  279.3 4.3 collective-permute-start.1
  288.0 3.2 copy-done.8
  292.0 2.8 slice_maximum_fusion
  294.8 3.5 copy.297
  298.3 3.5 copy.298
  305.5 7.0 %convert.10 = f32[2,1984,2,512]{3,0,2,1:T(2,128)S(1)} convert(bf16[2,1984,2,512]{3,0,2,1:T(2,128)(2,1)} %bitcast.290) | non-fusion elementwise | flops 4063232 | bytes 24379392 | tf_op jit(solution)/shard_map/convert_element_type | solution.py:41
  312.5 5.4 fusion.16
  325.9 8.2 %bitcast_convert_fusion = f32[2,992,2,512]{3,0,2,1:T(2,128)} fusion(bf16[2,992,2,512]{3,0,2,1:T(2,128)(2,1)} %bitcast.283), kind=kLoop, calls=%fused_computation.37 | loop fusion | flops 2031616 | bytes 12189696 | tf_op jit(solution)/shard_map/convert_element_type | solution.py:41
  334.0 5.6 fusion.24
  355.4 3.3 broadcast_in_dim.229
  358.7 4.8 reshape.711
  363.6 2.9 copy.300
  371.2 3.2 broadcast_in_dim.235
  374.4 4.8 reshape.715
  379.2 2.9 copy.307
  389.7 4.8 reshape.719
  394.5 2.9 copy.314
  397.4 4.3 collective-permute-start.3
  401.7 3.1 fusion.110
  408.1 3.1 fusion.109
  414.8 2.9 pad_maximum_fusion.12
  437.3 3.2 pad_maximum_fusion.5
  444.9 2.7 concatenate.75
  450.0 2.6 concatenate.78
  456.5 10.1 %pad_maximum_fusion = (bf16[2,2,768,8,64]{2,1,0,4,3:T(2,128)(2,1)}, bf16[2,2,768,8,64]{2,1,0,4,3:T(2,128)(2,1)}) fusion(bf16[2,2,256,8,64]{2,1,0,4,3:T(2,128)(2,1)} %concatenate.78, bf16[2,2,256,8,64]{2,1,0,4,3:T(2,128)(2,1)S(1)} %copy-done.13, bf16[2,2,256,8,64]{2,1,0,4,3:T(2,128)(2,1)} %concatenate.75, bf16[2,2,256,8,64]{2,1,0,4,3:T(2,128)(2,1)} %concatenate.82, ...), kind=kLoop, calls=%fused_computation.40 | loop fusion | flops 18874368 | bytes 12582912 | tf_op jit(solution)/shard_map/concatenate | solution.py:70
  466.6 29.8 %while.2 = (s32[]{:T(128)}, f32[2,2,256,8]{2,3,1,0:T(8,128)}, f32[2,2,256,8]{2,3,1,0:T(8,128)}, f32[2,2,256,8,64]{2,1,0,4,3:T(2,128)}, pred[2,2,768]{2,1,0:T(4,1...) while((s32[]{:T(128)}, f32[2,2,256,8]{2,3,1,0:T(8,128)}, ...), condition=%wide.region_3.4_spmd, body=%wide.region_0.3_spmd.sunk | while | flops 839901184 | bytes 80880952 | solution.py:89
  466.9 2.6 constant_dynamic-slice_fusion.11
  472.7 3.3 fusion.134
  476.1 3.1 fusion.133
  487.5 3.3 fusion.134
  490.9 3.1 fusion.133
  496.4 4.2 reshape.692
  506.4 3.4 fusion.46
  512.4 3.4 reshape.707
  517.7 3.1 fusion.19
  525.5 6.6 %fusion.41 = f32[2,256,8,64]{1,3,2,0:T(8,128)} fusion(f32[2,8,256,512]{3,2,1,0:T(8,128)} %copy-done.11, f32[2,8,256]{2,1,0:T(8,128)S(1)} %get-tuple-element.221, pred[2,512]{1,0:T(4,128)(4,1)S(1)} %copy-done.34, bf16[2,256,8,64]{1,3,2,0:T(8,128)(2,1)S(1)} %copy-done.21, bf16[2,256,8,64]{1,3,2,0:T(8,128)(2,1)S(1)} %copy-done.20), kind=kOutput, calls=%fused_computation.71 | convolution fusion | flops 281018368 | bytes 10503168 | tf_op jit(solution)/shard_map/while/body/eval_jaxpr/ghqk,gkhd->gqhd/dot_general | solution.py:54
  536.3 3.7 reshape.701
  542.9 6.6 %fusion.30 = bf16[1024,512]{0,1:T(8,128)(2,1)S(1)} fusion(f32[1024,512]{0,1:T(8,128)} %copy.314, f32[1024,512]{0,1:T(8,128)} %copy.307, f32[1024,512]{0,1:T(8,128)} %copy.300, f32[1024,512]{0,1:T(8,128)} %copy.293, f32[1024,512]{0,1:T(8,128)} %copy.280, f32[1024,512]{0,1:T(8,128)} %reshape.692, f32[1024,8]{0,1:T(8,128)S(1)} %get-tuple-element.156, ...), kind=kLoop, calls=%fused_computation.48 | loop fusion | flops 8912896 | bytes 13991936 | tf_op jit(solution)/shard_map/convert_element_type | solution.py:183
  549.5 2.6 convolution_convert_fusion
  552.2 17.6 %reduce-scatter.2.cloned.1.call-done = bf16[1024,512]{1,0:T(8,128)(2,1)} async-done(((bf16[1024,1024]{1,0:T(8,128)(2,1)}), bf16[1024,512]{1,0:T(8,128)(2,1)}) %reduce-scatter.2.cloned.1.call-update) | async-done | bytes 1048592 | tf_op jit(solution)/shard_map/reduce_scatter | solution.py:185
  (316 shorter events, 212.0 us)
Async XLA Ops:
  6.5 543.0 %copy-start = (bf16[512,1024]{1,0:T(8,128)(2,1)S(1)}, bf16[512,1024]{1,0:T(8,128)(2,1)}, u32[]{:S(2)}) copy-start(bf16[512,1024]{1,0:T(8,128)(2,1)} %param.9) | copy-start | bytes 3145732
  6.5 563.2 %reduce-scatter.2.cloned.1.call-start = ((), (), s32[]{:S(2)}) async-start(), calls=%async_computation.1 | async-start | bytes 3145728 | tf_op jit(solution)/shard_map/reduce_scatter | solution.py:185
  18.2 266.5 %collective-permute-start.35 = (bf16[2,128,512]{2,0,1:T(2,128)(2,1)}, bf16[2,128,512]{2,0,1:T(2,128)(2,1)}, u32[]{:S(2)}, u32[]{:S(2)}) collective-permute-start(bf16[2,128,512]{2,0,1:T(2,128)(2,1)} %fusion.86), channel_id=1, source_target_pairs={{30,0},{31,1}} | collective-permute-start | bytes 786440 | tf_op jit(solution)/shard_map/ppermute | solution.py:19
  19.5 259.7 %collective-permute-start.34 = (bf16[2,128,512]{2,0,1:T(2,128)(2,1)}, bf16[2,128,512]{2,0,1:T(2,128)(2,1)}, u32[]{:S(2)}, u32[]{:S(2)}) collective-permute-start(bf16[2,128,512]{2,0,1:T(2,128)(2,1)} %fusion.86), channel_id=1, source_target_pairs={{28,0},{30,2},{29,1},{31,3}} | collective-permute-start | bytes 786440 | tf_op jit(solution)/shard_map/ppermute | solution.py:19
  21.5 61.5 %collective-permute-start.8 = (bf16[2,128,512]{2,0,1:T(2,128)(2,1)}, bf16[2,128,512]{2,0,1:T(2,128)(2,1)}, u32[]{:S(2)}, u32[]{:S(2)}) collective-permute-start(bf16[2,128,512]{2,0,1:T(2,128)(2,1)} %fusion.86), channel_id=1, source_target_pairs={{0,26},{2,28},{4,30},{1,27},{3,29},{5,31}} | collective-permute-start | bytes 786440 | tf_op jit(solution)/shard_map/ppermute | solution.py:19
  22.8 57.8 %collective-permute-start.7 = (bf16[2,128,512]{2,0,1:T(2,128)(2,1)}, bf16[2,128,512]{2,0,1:T(2,128)(2,1)}, u32[]{:S(2)}, u32[]{:S(2)}) collective-permute-start(bf16[2,128,512]{2,0,1:T(2,128)(2,1)} %fusion.86), channel_id=1, source_target_pairs={{0,28},{2,30},{1,29},{3,31}} | collective-permute-start | bytes 786440 | tf_op jit(solution)/shard_map/ppermute | solution.py:19
  24.1 54.0 %collective-permute-start.6 = (bf16[2,128,512]{2,0,1:T(2,128)(2,1)}, bf16[2,128,512]{2,0,1:T(2,128)(2,1)}, u32[]{:S(2)}, u32[]{:S(2)}) collective-permute-start(bf16[2,128,512]{2,0,1:T(2,128)(2,1)} %fusion.86), channel_id=1, source_target_pairs={{0,30},{1,31}} | collective-permute-start | bytes 786440 | tf_op jit(solution)/shard_map/ppermute | solution.py:19
  39.1 17.4 %copy-start.5 = (bf16[1024,512]{1,0:T(8,128)(2,1)S(1)}, bf16[1024,512]{1,0:T(8,128)(2,1)}, u32[]{:S(2)}) copy-start(bf16[1024,512]{1,0:T(8,128)(2,1)} %param.8) | copy-start | bytes 3145732
  39.2 17.4 %copy-start.6 = (bf16[1024,512]{1,0:T(8,128)(2,1)S(1)}, bf16[1024,512]{1,0:T(8,128)(2,1)}, u32[]{:S(2)}) copy-start(bf16[1024,512]{1,0:T(8,128)(2,1)} %param.7) | copy-start | bytes 3145732
  62.4 11.9 %copy-start.25 = (bf16[64,512]{1,0:T(8,128)(2,1)S(1)}, bf16[64,512]{1,0:T(8,128)(2,1)}, u32[]{:S(2)}) copy-start(bf16[64,512]{1,0:T(8,128)(2,1)} %get-tuple-element.169) | copy-start | bytes 196612
  62.4 12.0 %copy-start.27 = (bf16[32,512]{1,0:T(8,128)(2,1)S(1)}, bf16[32,512]{1,0:T(8,128)(2,1)}, u32[]{:S(2)}) copy-start(bf16[32,512]{1,0:T(8,128)(2,1)} %convert_reduce_fusion.2) | copy-start | bytes 98308
  77.5 100.5 %copy-start.10 = (f32[2,128,2,512]{3,0,2,1:T(2,128)S(1)}, f32[2,128,2,512]{3,0,2,1:T(2,128)}, u32[]{:S(2)}) copy-start(f32[2,128,2,512]{3,0,2,1:T(2,128)} %copy-done.9) | copy-start | bytes 3145732
  78.1 13.2 %collective-permute-start.9 = (bf16[2,128,512]{2,0,1:T(2,128)(2,1)}, bf16[2,128,512]{2,0,1:T(2,128)(2,1)S(1)}, u32[]{:S(2)}, u32[]{:S(2)}) collective-permute-start(bf16[2,128,512]{2,0,1:T(2,128)(2,1)} %fusion.86), channel_id=1, source_target_pairs={{0,24},{2,26},{4,28},{6,30},{1,25},{3,27},{5,29},{7,31}} | collective-permute-start | bytes 786440 | tf_op jit(solution)/shard_map/ppermute | solution.py:19
  80.6 15.6 %collective-permute-start.10 = (bf16[2,128,512]{2,0,1:T(2,128)(2,1)}, bf16[2,128,512]{2,0,1:T(2,128)(2,1)S(1)}, u32[]{:S(2)}, u32[]{:S(2)}) collective-permute-start(bf16[2,128,512]{2,0,1:T(2,128)(2,1)} %fusion.86), channel_id=1, source_target_pairs={{0,22},{2,24},{4,26},{6,28},{8,30},{1,23},{3,25},{5,27},{7,29},{9,... | collective-permute-start | bytes 786440 | tf_op jit(solution)/shard_map/ppermute | solution.py:19
  83.0 44.0 %collective-permute-start.11 = (bf16[2,128,512]{2,0,1:T(2,128)(2,1)}, bf16[2,128,512]{2,0,1:T(2,128)(2,1)S(1)}, u32[]{:S(2)}, u32[]{:S(2)}) collective-permute-start(bf16[2,128,512]{2,0,1:T(2,128)(2,1)} %fusion.86), channel_id=1, source_target_pairs={{0,20},{2,22},{4,24},{6,26},{8,28},{10,30},{1,21},{3,23},{5,25},{7... | collective-permute-start | bytes 786440 | tf_op jit(solution)/shard_map/ppermute | solution.py:19
  91.4 41.4 %collective-permute-start.12 = (bf16[2,128,512]{2,0,1:T(2,128)(2,1)}, bf16[2,128,512]{2,0,1:T(2,128)(2,1)S(1)}, u32[]{:S(2)}, u32[]{:S(2)}) collective-permute-start(bf16[2,128,512]{2,0,1:T(2,128)(2,1)} %fusion.86), channel_id=1, source_target_pairs={{0,18},{2,20},{4,22},{6,24},{8,26},{10,28},{12,30},{1,19},{3,21},{... | collective-permute-start | bytes 786440 | tf_op jit(solution)/shard_map/ppermute | solution.py:19
  96.2 38.1 %collective-permute-start.13 = (bf16[2,128,512]{2,0,1:T(2,128)(2,1)}, bf16[2,128,512]{2,0,1:T(2,128)(2,1)S(1)}, u32[]{:S(2)}, u32[]{:S(2)}) collective-permute-start(bf16[2,128,512]{2,0,1:T(2,128)(2,1)} %fusion.86), channel_id=1, source_target_pairs={{0,16},{2,18},{4,20},{6,22},{8,24},{10,26},{12,28},{14,30},{1,17},... | collective-permute-start | bytes 786440 | tf_op jit(solution)/shard_map/ppermute | solution.py:19
  127.1 11.2 %collective-permute-start.14 = (bf16[2,128,512]{2,0,1:T(2,128)(2,1)}, bf16[2,128,512]{2,0,1:T(2,128)(2,1)S(1)}, u32[]{:S(2)}, u32[]{:S(2)}) collective-permute-start(bf16[2,128,512]{2,0,1:T(2,128)(2,1)} %fusion.86), channel_id=1, source_target_pairs={{0,14},{2,16},{4,18},{6,20},{8,22},{10,24},{12,26},{14,28},{16,30}... | collective-permute-start | bytes 786440 | tf_op jit(solution)/shard_map/ppermute | solution.py:19
  132.8 16.7 %collective-permute-start.15 = (bf16[2,128,512]{2,0,1:T(2,128)(2,1)}, bf16[2,128,512]{2,0,1:T(2,128)(2,1)S(1)}, u32[]{:S(2)}, u32[]{:S(2)}) collective-permute-start(bf16[2,128,512]{2,0,1:T(2,128)(2,1)} %fusion.86), channel_id=1, source_target_pairs={{0,12},{2,14},{4,16},{6,18},{8,20},{10,22},{12,24},{14,26},{16,28}... | collective-permute-start | bytes 786440 | tf_op jit(solution)/shard_map/ppermute | solution.py:19
  134.3 21.6 %collective-permute-start.16 = (bf16[2,128,512]{2,0,1:T(2,128)(2,1)}, bf16[2,128,512]{2,0,1:T(2,128)(2,1)S(1)}, u32[]{:S(2)}, u32[]{:S(2)}) collective-permute-start(bf16[2,128,512]{2,0,1:T(2,128)(2,1)} %fusion.86), channel_id=1, source_target_pairs={{0,10},{2,12},{4,14},{6,16},{8,18},{10,20},{12,22},{14,24},{16,26}... | collective-permute-start | bytes 786440 | tf_op jit(solution)/shard_map/ppermute | solution.py:19
  138.2 19.2 %collective-permute-start.17 = (bf16[2,128,512]{2,0,1:T(2,128)(2,1)}, bf16[2,128,512]{2,0,1:T(2,128)(2,1)S(1)}, u32[]{:S(2)}, u32[]{:S(2)}) collective-permute-start(bf16[2,128,512]{2,0,1:T(2,128)(2,1)} %fusion.86), channel_id=1, source_target_pairs={{0,8},{2,10},{4,12},{6,14},{8,16},{10,18},{12,20},{14,22},{16,24},... | collective-permute-start | bytes 786440 | tf_op jit(solution)/shard_map/ppermute | solution.py:19
  149.5 17.4 %collective-permute-start.18 = (bf16[2,128,512]{2,0,1:T(2,128)(2,1)}, bf16[2,128,512]{2,0,1:T(2,128)(2,1)S(1)}, u32[]{:S(2)}, u32[]{:S(2)}) collective-permute-start(bf16[2,128,512]{2,0,1:T(2,128)(2,1)} %fusion.86), channel_id=1, source_target_pairs={{0,6},{2,8},{4,10},{6,12},{8,14},{10,16},{12,18},{14,20},{16,22},{... | collective-permute-start | bytes 786440 | tf_op jit(solution)/shard_map/ppermute | solution.py:19
  155.9 12.6 %collective-permute-start.19 = (bf16[2,128,512]{2,0,1:T(2,128)(2,1)}, bf16[2,128,512]{2,0,1:T(2,128)(2,1)S(1)}, u32[]{:S(2)}, u32[]{:S(2)}) collective-permute-start(bf16[2,128,512]{2,0,1:T(2,128)(2,1)} %fusion.86), channel_id=1, source_target_pairs={{0,4},{2,6},{4,8},{6,10},{8,12},{10,14},{12,16},{14,18},{16,20},{1... | collective-permute-start | bytes 786440 | tf_op jit(solution)/shard_map/ppermute | solution.py:19
  157.4 15.4 %collective-permute-start.20 = (bf16[2,128,512]{2,0,1:T(2,128)(2,1)}, bf16[2,128,512]{2,0,1:T(2,128)(2,1)S(1)}, u32[]{:S(2)}, u32[]{:S(2)}) collective-permute-start(bf16[2,128,512]{2,0,1:T(2,128)(2,1)} %fusion.86), channel_id=1, source_target_pairs={{0,2},{2,4},{4,6},{6,8},{8,10},{10,12},{12,14},{14,16},{16,18},{18... | collective-permute-start | bytes 786440 | tf_op jit(solution)/shard_map/ppermute | solution.py:19
  166.9 25.4 %collective-permute-start.23 = (bf16[2,128,512]{2,0,1:T(2,128)(2,1)}, bf16[2,128,512]{2,0,1:T(2,128)(2,1)S(1)}, u32[]{:S(2)}, u32[]{:S(2)}) collective-permute-start(bf16[2,128,512]{2,0,1:T(2,128)(2,1)} %fusion.86), channel_id=1, source_target_pairs={{6,0},{8,2},{10,4},{12,6},{14,8},{16,10},{18,12},{20,14},{22,16},{... | collective-permute-start | bytes 786440 | tf_op jit(solution)/shard_map/ppermute | solution.py:19
  168.5 22.3 %collective-permute-start.22 = (bf16[2,128,512]{2,0,1:T(2,128)(2,1)}, bf16[2,128,512]{2,0,1:T(2,128)(2,1)S(1)}, u32[]{:S(2)}, u32[]{:S(2)}) collective-permute-start(bf16[2,128,512]{2,0,1:T(2,128)(2,1)} %fusion.86), channel_id=1, source_target_pairs={{4,0},{6,2},{8,4},{10,6},{12,8},{14,10},{16,12},{18,14},{20,16},{2... | collective-permute-start | bytes 786440 | tf_op jit(solution)/shard_map/ppermute | solution.py:19
  172.8 15.3 %collective-permute-start.21 = (bf16[2,128,512]{2,0,1:T(2,128)(2,1)}, bf16[2,128,512]{2,0,1:T(2,128)(2,1)S(1)}, u32[]{:S(2)}, u32[]{:S(2)}) collective-permute-start(bf16[2,128,512]{2,0,1:T(2,128)(2,1)} %fusion.86), channel_id=1, source_target_pairs={{2,0},{4,2},{6,4},{8,6},{10,8},{12,10},{14,12},{16,14},{18,16},{20... | collective-permute-start | bytes 786440 | tf_op jit(solution)/shard_map/ppermute | solution.py:19
  188.1 7.5 %collective-permute-start.24 = (bf16[2,128,512]{2,0,1:T(2,128)(2,1)}, bf16[2,128,512]{2,0,1:T(2,128)(2,1)S(1)}, u32[]{:S(2)}, u32[]{:S(2)}) collective-permute-start(bf16[2,128,512]{2,0,1:T(2,128)(2,1)} %fusion.86), channel_id=1, source_target_pairs={{8,0},{10,2},{12,4},{14,6},{16,8},{18,10},{20,12},{22,14},{24,16},... | collective-permute-start | bytes 786440 | tf_op jit(solution)/shard_map/ppermute | solution.py:19
  190.8 10.9 %collective-permute-start.25 = (bf16[2,128,512]{2,0,1:T(2,128)(2,1)}, bf16[2,128,512]{2,0,1:T(2,128)(2,1)S(1)}, u32[]{:S(2)}, u32[]{:S(2)}) collective-permute-start(bf16[2,128,512]{2,0,1:T(2,128)(2,1)} %fusion.86), channel_id=1, source_target_pairs={{10,0},{12,2},{14,4},{16,6},{18,8},{20,10},{22,12},{24,14},{26,16}... | collective-permute-start | bytes 786440 | tf_op jit(solution)/shard_map/ppermute | solution.py:19
  192.3 15.0 %collective-permute-start.26 = (bf16[2,128,512]{2,0,1:T(2,128)(2,1)}, bf16[2,128,512]{2,0,1:T(2,128)(2,1)S(1)}, u32[]{:S(2)}, u32[]{:S(2)}) collective-permute-start(bf16[2,128,512]{2,0,1:T(2,128)(2,1)} %fusion.86), channel_id=1, source_target_pairs={{12,0},{14,2},{16,4},{18,6},{20,8},{22,10},{24,12},{26,14},{28,16}... | collective-permute-start | bytes 786440 | tf_op jit(solution)/shard_map/ppermute | solution.py:19
  195.6 18.3 %collective-permute-start.27 = (bf16[2,128,512]{2,0,1:T(2,128)(2,1)}, bf16[2,128,512]{2,0,1:T(2,128)(2,1)S(1)}, u32[]{:S(2)}, u32[]{:S(2)}) collective-permute-start(bf16[2,128,512]{2,0,1:T(2,128)(2,1)} %fusion.86), channel_id=1, source_target_pairs={{14,0},{16,2},{18,4},{20,6},{22,8},{24,10},{26,12},{28,14},{30,16}... | collective-permute-start | bytes 786440 | tf_op jit(solution)/shard_map/ppermute | solution.py:19
  201.7 16.4 %collective-permute-start.28 = (bf16[2,128,512]{2,0,1:T(2,128)(2,1)}, bf16[2,128,512]{2,0,1:T(2,128)(2,1)S(1)}, u32[]{:S(2)}, u32[]{:S(2)}) collective-permute-start(bf16[2,128,512]{2,0,1:T(2,128)(2,1)} %fusion.86), channel_id=1, source_target_pairs={{16,0},{18,2},{20,4},{22,6},{24,8},{26,10},{28,12},{30,14},{17,1},... | collective-permute-start | bytes 786440 | tf_op jit(solution)/shard_map/ppermute | solution.py:19
  207.3 39.8 %collective-permute-start.29 = (bf16[2,128,512]{2,0,1:T(2,128)(2,1)}, bf16[2,128,512]{2,0,1:T(2,128)(2,1)S(1)}, u32[]{:S(2)}, u32[]{:S(2)}) collective-permute-start(bf16[2,128,512]{2,0,1:T(2,128)(2,1)} %fusion.86), channel_id=1, source_target_pairs={{18,0},{20,2},{22,4},{24,6},{26,8},{28,10},{30,12},{19,1},{21,3},{... | collective-permute-start | bytes 786440 | tf_op jit(solution)/shard_map/ppermute | solution.py:19
  213.9 38.9 %collective-permute-start.30 = (bf16[2,128,512]{2,0,1:T(2,128)(2,1)}, bf16[2,128,512]{2,0,1:T(2,128)(2,1)S(1)}, u32[]{:S(2)}, u32[]{:S(2)}) collective-permute-start(bf16[2,128,512]{2,0,1:T(2,128)(2,1)} %fusion.86), channel_id=1, source_target_pairs={{20,0},{22,2},{24,4},{26,6},{28,8},{30,10},{21,1},{23,3},{25,5},{2... | collective-permute-start | bytes 786440 | tf_op jit(solution)/shard_map/ppermute | solution.py:19
  218.1 52.5 %collective-permute-start.31 = (bf16[2,128,512]{2,0,1:T(2,128)(2,1)}, bf16[2,128,512]{2,0,1:T(2,128)(2,1)S(1)}, u32[]{:S(2)}, u32[]{:S(2)}) collective-permute-start(bf16[2,128,512]{2,0,1:T(2,128)(2,1)} %fusion.86), channel_id=1, source_target_pairs={{22,0},{24,2},{26,4},{28,6},{30,8},{23,1},{25,3},{27,5},{29,7},{31... | collective-permute-start | bytes 786440 | tf_op jit(solution)/shard_map/ppermute | solution.py:19
  247.2 25.5 %collective-permute-start.32 = (bf16[2,128,512]{2,0,1:T(2,128)(2,1)}, bf16[2,128,512]{2,0,1:T(2,128)(2,1)S(1)}, u32[]{:S(2)}, u32[]{:S(2)}) collective-permute-start(bf16[2,128,512]{2,0,1:T(2,128)(2,1)} %fusion.86), channel_id=1, source_target_pairs={{24,0},{26,2},{28,4},{30,6},{25,1},{27,3},{29,5},{31,7}} | collective-permute-start | bytes 786440 | tf_op jit(solution)/shard_map/ppermute | solution.py:19
  252.8 24.3 %collective-permute-start.33 = (bf16[2,128,512]{2,0,1:T(2,128)(2,1)}, bf16[2,128,512]{2,0,1:T(2,128)(2,1)S(1)}, u32[]{:S(2)}, u32[]{:S(2)}) collective-permute-start(bf16[2,128,512]{2,0,1:T(2,128)(2,1)} %fusion.86), channel_id=1, source_target_pairs={{26,0},{28,2},{30,4},{27,1},{29,3},{31,5}} | collective-permute-start | bytes 786440 | tf_op jit(solution)/shard_map/ppermute | solution.py:19
  270.5 126.9 %collective-permute-start.5 = (bf16[2,256,512]{2,0,1:T(2,128)(2,1)}, bf16[2,256,512]{2,0,1:T(2,128)(2,1)}, u32[]{:S(2)}, u32[]{:S(2)}) collective-permute-start(bf16[2,256,512]{2,0,1:T(2,128)(2,1)} %fusion.126), channel_id=1, source_target_pairs={{2,0},{4,2},{6,4},{8,6},{10,8},{12,10},{14,12},{16,14},{18,16},{20... | collective-permute-start | bytes 1572872 | tf_op jit(solution)/shard_map/ppermute | solution.py:32
  272.7 135.3 %collective-permute-start.4 = (bf16[2,256,512]{2,0,1:T(2,128)(2,1)}, bf16[2,256,512]{2,0,1:T(2,128)(2,1)}, u32[]{:S(2)}, u32[]{:S(2)}) collective-permute-start(bf16[2,256,512]{2,0,1:T(2,128)(2,1)} %fusion.126), channel_id=1, source_target_pairs={{0,2},{2,4},{4,6},{6,8},{8,10},{10,12},{12,14},{14,16},{16,18},{18... | collective-permute-start | bytes 1572872 | tf_op jit(solution)/shard_map/ppermute | solution.py:30
  277.1 160.2 %collective-permute-start = (bf16[2,256,512]{2,1,0:T(8,128)(2,1)}, bf16[2,256,512]{2,1,0:T(8,128)(2,1)}, u32[]{:S(2)}, u32[]{:S(2)}) collective-permute-start(bf16[2,256,512]{2,1,0:T(8,128)(2,1)} %get-tuple-element.185), channel_id=1, source_target_pairs={{0,2},{2,4},{4,6},{6,8},{8,10},{10,12},{12,14},{14,16},{16,18},{18... | collective-permute-start | bytes 1572872 | tf_op jit(solution)/shard_map/ppermute | solution.py:30
  279.3 158.0 %collective-permute-start.1 = (bf16[2,256,512]{2,1,0:T(8,128)(2,1)}, bf16[2,256,512]{2,1,0:T(8,128)(2,1)}, u32[]{:S(2)}, u32[]{:S(2)}) collective-permute-start(bf16[2,256,512]{2,1,0:T(8,128)(2,1)} %get-tuple-element.186), channel_id=1, source_target_pairs={{2,0},{4,2},{6,4},{8,6},{10,8},{12,10},{14,12},{16,14},{18,16},{20... | collective-permute-start | bytes 1572872 | tf_op jit(solution)/shard_map/ppermute | solution.py:32
  284.7 130.1 %collective-permute-start.2 = (bf16[2,256,512]{2,1,0:T(8,128)(2,1)}, bf16[2,256,512]{2,1,0:T(8,128)(2,1)}, u32[]{:S(2)}, u32[]{:S(2)}) collective-permute-start(bf16[2,256,512]{2,1,0:T(8,128)(2,1)} %get-tuple-element.197), channel_id=1, source_target_pairs={{0,2},{2,4},{4,6},{6,8},{8,10},{10,12},{12,14},{14,16},{16,18},{18... | collective-permute-start | bytes 1572872 | tf_op jit(solution)/shard_map/ppermute | solution.py:30
  288.0 3.2 copy-start.8
  291.2 10.5 %copy-start.28 = (bf16[128,1,512]{0,2,1:T(8,128)(2,1)S(1)}, bf16[128,1,512]{0,2,1:T(8,128)(2,1)}, u32[]{:S(2)}) copy-start(bf16[128,1,512]{0,2,1:T(8,128)(2,1)} %copy.296) | copy-start | bytes 393220
  397.4 17.4 %collective-permute-start.3 = (bf16[2,256,512]{2,1,0:T(8,128)(2,1)}, bf16[2,256,512]{2,1,0:T(8,128)(2,1)}, u32[]{:S(2)}, u32[]{:S(2)}) collective-permute-start(bf16[2,256,512]{2,1,0:T(8,128)(2,1)} %get-tuple-element.198), channel_id=1, source_target_pairs={{2,0},{4,2},{6,4},{8,6},{10,8},{12,10},{14,12},{16,14},{18,16},{20... | collective-permute-start | bytes 1572872 | tf_op jit(solution)/shard_map/ppermute | solution.py:32
  440.5 3.2 copy-start.15
  443.6 9.0 %copy-start.14 = (bf16[1,1024,512]{2,1,0:T(8,128)(2,1)S(1)}, bf16[1,1024,512]{2,1,0:T(8,128)(2,1)}, u32[]{:S(2)}) copy-start(bf16[1,1024,512]{2,1,0:T(8,128)(2,1)} %get-tuple-element.184) | copy-start | bytes 3145732
  447.6 8.9 %copy-start.13 = (bf16[2,2,256,8,64]{2,1,0,4,3:T(2,128)(2,1)S(1)}, bf16[2,2,256,8,64]{2,1,0,4,3:T(2,128)(2,1)}, u32[]{:S(2)}) copy-start(bf16[2,2,256,8,64]{2,1,0,4,3:T(2,128)(2,1)} %concatenate.76) | copy-start | bytes 3145732
  456.5 10.1 %copy-start.7 = (bf16[2,2,256,8,64]{2,4,3,1,0:T(8,128)(2,1)S(1)}, bf16[2,2,256,8,64]{2,4,3,1,0:T(8,128)(2,1)}, u32[]{:S(2)}) copy-start(bf16[2,2,256,8,64]{2,4,3,1,0:T(8,128)(2,1)} %copy.257) | copy-start | bytes 3145732
  476.1 3.2 copy-start.29
  476.1 3.2 copy-start.32
  476.1 3.2 copy-start.17
  490.8 3.2 copy-start.29
  490.8 3.2 copy-start.17
  496.4 4.2 copy-start.24
  496.4 4.2 copy-start.26
  496.4 4.2 copy-start.35
  501.6 4.7 copy-start.22
  501.7 4.7 copy-start.23
  512.4 5.3 copy-start.34
  520.7 3.2 copy-start.11
  520.7 4.8 copy-start.20
  520.7 4.8 copy-start.21
  536.3 5.7 copy-start.31
  (16 other events, 28.2 us)
Sparse Core Ops, SparseCore 0:
  552.3 17.4 reduce-scatter.1
where the time goes:
time: 586 us; the launch traced here: 577 us
  local copies, waits for them, and re-layouts  214 us (37%)
  starting transfers between devices  135 us (23%)
  waiting for transfers between devices  91.8 us (16%)
  other arithmetic  84.4 us (14%)
  matrix products  36.2 us (6%)
  between operations  14.9 us (3%)
    ppermute x30, starting transfers between devices, shifted(): lax.ppermute(value, axis, [(source, source + steps) for source in range(l...  116 us
    ppermute x30, waiting for transfers between devices, shifted(): lax.ppermute(value, axis, [(source, source + steps) for source in range(l...  74.2 us
    reshape x10, local copies, waits for them, and re-layouts, local(): numerator = jnp.repeat(numerator, factor, axis=0)  34.1 us
    unnamed x89, local copies, waits for them, and re-layouts  24.3 us
    convert_element_type x12, other arithmetic, coarsen(): ((widened[..., 0, :] + widened[..., 1, :]) * 0.5).astype(jnp.bfloat16)  23.7 us
    slice x10, local copies, waits for them, and re-layouts, local_level(): value_blocks[offset:offset + blocks]  22.7 us
    dot_general x7, matrix products, attend_groups(): jnp.einsum('ghqk,gkhd->gqhd', weights.astype(jnp.bfloat16), value_part, p...  20.8 us
    convert_element_type x5, other arithmetic, coarsen(): rows_in.astype(jnp.float32)  18 us
  transfers between devices with their start and end apart: 37, of which 13 were waited for; matrix products, arithmetic and copies ran while one was open for 35% of the time, Pallas kernels for 0%

commit v1 on v0

v1 whole, which is shorter than its diff:
```python
import functools
import math

import jax
import jax.numpy as jnp
from jax import lax
from jax.experimental import pallas as pl
from jax.experimental.pallas import tpu as pltpu
from jax.sharding import PartitionSpec as P

HEAD_DIM = 64
BLOCK = 256
LEVELS = 6
LOG_TWO = 0.6931471805599453
NEG_LARGE = -1e30
LANES = 128
MESH = pl.DeviceIdType.MESH
BF16 = jnp.bfloat16
F32 = jnp.float32


def pool(x):
    rows = x.shape[0]
    r = lax.broadcasted_iota(jnp.int32, (rows // 2, rows), 0)
    c = lax.broadcasted_iota(jnp.int32, (rows // 2, rows), 1)
    mat = jnp.where((c == 2 * r) | (c == 2 * r + 1), 0.5, 0.0).astype(BF16)
    return jnp.dot(mat, x, preferred_element_type=F32).astype(BF16)


def kernel(n_seq, tok, pairs, q_hbm, k_hbm, v_hbm, w_hbm, o_ref, *scratch):
    scratch = list(scratch)

    def take(count):
        out = scratch[:count]
        del scratch[:count]
        return out

    kv = take(LEVELS)
    qs = take(LEVELS)
    nums = take(LEVELS)
    tots = take(LEVELS)
    mxs = take(LEVELS)
    tmp, att, w_s, psend, precv, load_sem, send_sem, recv_sem, psend_sem, precv_sem = scratch

    me = lax.axis_index("seq")
    head = lax.axis_index("head")
    rows_of = [tok >> l for l in range(LEVELS)]
    span_of = [max(1, BLOCK // r) for r in rows_of]
    half = o_ref.shape[1]

    loads = []
    for p in range(pairs):
        cols = pl.ds(p * LANES, LANES)
        loads.append(pltpu.make_async_copy(
            k_hbm.at[:, cols], kv[0].at[0, p, pl.ds(BLOCK, tok)], load_sem.at[0, p]))
        loads.append(pltpu.make_async_copy(
            v_hbm.at[:, cols], kv[0].at[1, p, pl.ds(BLOCK, tok)], load_sem.at[1, p]))
        loads.append(pltpu.make_async_copy(q_hbm.at[:, cols], qs[0].at[p], load_sem.at[2, p]))
    w_load = pltpu.make_async_copy(w_hbm, w_s, load_sem.at[3, 0])
    for c in loads:
        c.start()
    w_load.start()

    top = span_of[-1]
    top_block = me // top
    top_blocks = n_seq // top
    barrier = pltpu.get_barrier_semaphore()
    pl.semaphore_signal(barrier, inc=1, device_id={"head": 1 - head}, device_id_type=MESH)
    for delta in (-1, 0, 1):
        there = top_block + delta

        @pl.when((there >= 0) & (there < top_blocks))
        def _():
            for j in range(top):
                other = there * top + j

                @pl.when(other != me)
                def _():
                    pl.semaphore_signal(
                        barrier, inc=1, device_id={"seq": other}, device_id_type=MESH)

    exists = []
    for l in range(LEVELS):
        block = me // span_of[l]
        has_left = block >= 1
        has_right = block + 1 < n_seq // span_of[l]
        exists.append((has_left, has_right))
        r = rows_of[l]

        @pl.when(jnp.logical_not(has_left))
        def _():
            kv[l][:, :, pl.ds(0, BLOCK), :] = jnp.zeros((2, pairs, BLOCK, LANES), BF16)

        @pl.when(jnp.logical_not(has_right))
        def _():
            kv[l][:, :, pl.ds(BLOCK + r, BLOCK), :] = jnp.zeros((2, pairs, BLOCK, LANES), BF16)

    around = jnp.minimum(top_block, 1) + jnp.minimum(top_blocks - 1 - top_block, 1)
    pl.semaphore_wait(barrier, top + top * around)

    def copies(l, side):
        r, n = rows_of[l], span_of[l]
        block, place = me // n, lax.rem(me, n)
        if r >= BLOCK:
            length = BLOCK if l == 0 else BLOCK // 2
            if side == 1:
                src, dst = BLOCK + r - BLOCK, 0
            else:
                src = BLOCK + BLOCK - length
                dst = BLOCK + r + BLOCK - length
        else:
            length = r
            src = BLOCK
            dst = place * r + (0 if side == 1 else BLOCK + r)
            dst = pl.multiple_of(dst, r)
        out = []
        for j in range(n):
            target = (block + (1 if side == 1 else -1)) * n + j
            out.append(pltpu.make_async_remote_copy(
                src_ref=kv[l].at[:, :, pl.ds(src, length)],
                dst_ref=kv[l].at[:, :, pl.ds(dst, length)],
                send_sem=send_sem.at[l, side, j],
                recv_sem=recv_sem.at[l, 1 - side],
                device_id={"seq": target},
                device_id_type=MESH))
        return out

    def start(l):
        for side in (0, 1):
            @pl.when(exists[l][side])
            def _():
                for c in copies(l, side):
                    c.start()

    def wait(l):
        r = rows_of[l]
        for side in (0, 1):
            length = BLOCK // 2 if (r >= BLOCK and l > 0) else BLOCK
            if side == 0:
                at = 0
            else:
                at = BLOCK + r + BLOCK - length

            @pl.when(exists[l][side])
            def _():
                region = kv[l].at[:, :, pl.ds(at, length)]
                pltpu.make_async_copy(region, region, recv_sem.at[l, side]).wait()

    for c in loads:
        c.wait()
    start(0)

    for l in range(1, LEVELS):
        r = rows_of[l]
        step = min(BLOCK, 2 * r)

        def coarse(p, _, l=l, r=r, step=step):
            for at in range(0, 2 * r, step):
                for s in range(2):
                    kv[l][s, p, pl.ds(BLOCK + at // 2, step // 2), :] = pool(
                        kv[l - 1][s, p, pl.ds(BLOCK + at, step), :])
                qs[l][p, pl.ds(at // 2, step // 2), :] = pool(qs[l - 1][p, pl.ds(at, step), :])
            return 0

        lax.fori_loop(0, pairs, coarse, 0)
        start(l)

    lane = lax.broadcasted_iota(jnp.int32, (1, LANES), 1)
    low = lane < HEAD_DIM
    masks = [jnp.where(low, 1.0, 0.0).astype(BF16), jnp.where(low, 0.0, 1.0).astype(BF16)]
    scale = HEAD_DIM ** -0.5

    def bias_of(valid):
        return jnp.where(valid, 0.0, NEG_LARGE).astype(F32)

    def attend(l, j, p):
        r = rows_of[l]
        size = min(BLOCK, r)
        has_left, has_right = exists[l]
        blocks = max(1, r // BLOCK)
        if r >= BLOCK:
            left_at, right_at = j * BLOCK, (j + 2) * BLOCK
        else:
            left_at, right_at = 0, BLOCK + r
        left_bias = bias_of(has_left) if j == 0 else None
        right_bias = bias_of(has_right) if j == blocks - 1 else None
        if l == 0:
            segments = [(left_at, left_bias), (left_at + BLOCK, None), (right_at, right_bias)]
        else:
            segments = [(left_at, left_bias), (right_at, right_bias)]
        q = qs[l][p, pl.ds(j * BLOCK, size), :]
        ks = [kv[l][0, p, pl.ds(at, BLOCK), :] for at, _ in segments]
        vs = [kv[l][1, p, pl.ds(at, BLOCK), :] for at, _ in segments]
        accs, peaks = [], []
        for e in (0, 1):
            mine = masks[e]
            other = masks[1 - e]
            q_e = q * (mine * scale) + other
            k_e = []
            for (at, bias), k in zip(segments, ks):
                k = k * mine
                if bias is not None:
                    k = k + (other.astype(F32) * bias).astype(BF16)
                k_e.append(k)
            k_e = jnp.concatenate(k_e, axis=0)
            v_e = jnp.concatenate([v * mine + other for v in vs], axis=0)
            s = lax.dot_general(q_e, k_e, (((1,), (1,)), ((), ())), preferred_element_type=F32)
            peak = jnp.max(s, axis=1, keepdims=True)
            weights = jnp.exp(s - peak).astype(BF16)
            accs.append(jnp.dot(weights, v_e, preferred_element_type=F32))
            peaks.append(peak)
        at = pl.ds(j * BLOCK, size)
        nums[l][p, at, :] = jnp.where(low, accs[0], accs[1])
        tots[l][p, at, :] = pltpu.roll(jnp.where(low, accs[1], accs[0]), HEAD_DIM, 1)
        mxs[l][p, at, :] = jnp.where(low, peaks[0], peaks[1]) + l * LOG_TWO

    def phase(l, which):
        def body(p, _):
            for j in which:
                attend(l, j, p)
            return 0

        lax.fori_loop(0, pairs, body, 0)

    def near(l):
        r, below = rows_of[l], rows_of[l - 1]

        def body(p, _):
            for s in range(2):
                kv[l][s, p, pl.ds(BLOCK // 2, BLOCK // 2), :] = pool(
                    kv[l - 1][s, p, pl.ds(0, BLOCK), :])
                kv[l][s, p, pl.ds(BLOCK + r, BLOCK // 2), :] = pool(
                    kv[l - 1][s, p, pl.ds(BLOCK + below, BLOCK), :])
            return 0

        lax.fori_loop(0, pairs, body, 0)

    blocks0 = max(1, tok // BLOCK)
    inner = list(range(1, blocks0 - 1))
    outer = [j for j in range(blocks0) if j not in inner]
    for j in inner:
        phase(0, [j])
    wait(0)
    for j in outer:
        phase(0, [j])
    for l in range(1, LEVELS):
        wait(l)
        if rows_of[l] >= BLOCK:
            near(l)
        for j in range(max(1, rows_of[l] // BLOCK)):
            phase(l, [j])

    def join(p, _):
        cur = (nums[-1][p], tots[-1][p], mxs[-1][p])
        for l in range(LEVELS - 2, -1, -1):
            r = rows_of[l]
            for i, x in enumerate(cur):
                tmp[i, pl.ds(0, r // 2, stride=2), :] = x
                tmp[i, pl.ds(1, r // 2, stride=2), :] = x
            num, tot, peak = (tmp[i, pl.ds(0, r), :] for i in range(3))
            peak_l = mxs[l][p]
            newest = jnp.maximum(peak, peak_l)
            keep = jnp.exp(peak - newest)
            fresh = jnp.exp(peak_l - newest)
            cur = (num * keep + nums[l][p] * fresh, tot * keep + tots[l][p] * fresh, newest)
        att[:, pl.ds(pl.multiple_of(p * LANES, LANES), LANES)] = (cur[0] / cur[1]).astype(BF16)
        return 0

    lax.fori_loop(0, pairs, join, 0)

    w_load.wait()
    chunk = min(BLOCK, tok)
    chunks = tok // chunk
    other_cols = pl.ds(pl.multiple_of((1 - head) * half, half), half)
    own_cols = pl.ds(pl.multiple_of(head * half, half), half)

    def part_copy(c):
        at = pl.ds(c * chunk, chunk)
        return pltpu.make_async_remote_copy(
            src_ref=psend.at[at], dst_ref=precv.at[at],
            send_sem=psend_sem.at[c], recv_sem=precv_sem.at[c],
            device_id={"head": 1 - head}, device_id_type=MESH)

    for c in range(chunks):
        at = pl.ds(c * chunk, chunk)
        psend[at, :] = jnp.dot(
            att[at, :], w_s[:, other_cols], preferred_element_type=F32).astype(BF16)
        part_copy(c).start()
    for c in range(chunks):
        at = pl.ds(c * chunk, chunk)
        own = jnp.dot(att[at, :], w_s[:, own_cols], preferred_element_type=F32).astype(BF16)
        part_copy(c).wait_recv()
        o_ref[at, :] = (own.astype(F32) + precv[at, :].astype(F32)).astype(BF16)
    for c in range(chunks):
        part_copy(c).wait_send()
    for l in range(LEVELS):
        for side in (0, 1):
            @pl.when(exists[l][side])
            def _():
                for c in copies(l, side):
                    c.wait_send()


def local(n_seq, queries, key_rows, value_rows, out_weight):
    tok, columns = queries.shape
    pairs = columns // LANES
    width = out_weight.shape[1]
    half = width // 2
    rows_of = [tok >> l for l in range(LEVELS)]
    top = max(1, BLOCK // rows_of[-1])
    chunks = tok // min(BLOCK, tok)
    results = [pltpu.VMEM((pairs, r, LANES), F32) for r in rows_of]
    scratch = (
        [pltpu.VMEM((2, pairs, r + 2 * BLOCK, LANES), BF16) for r in rows_of]
        + [pltpu.VMEM((pairs, r, LANES), BF16) for r in rows_of]
        + results * 3
        + [
            pltpu.VMEM((3, tok, LANES), F32),
            pltpu.VMEM((tok, columns), BF16),
            pltpu.VMEM(out_weight.shape, BF16),
            pltpu.VMEM((tok, half), BF16),
            pltpu.VMEM((tok, half), BF16),
            pltpu.SemaphoreType.DMA((4, pairs)),
            pltpu.SemaphoreType.DMA((LEVELS, 2, top)),
            pltpu.SemaphoreType.DMA((LEVELS, 2)),
            pltpu.SemaphoreType.DMA((chunks,)),
            pltpu.SemaphoreType.DMA((chunks,)),
        ]
    )
    return pl.pallas_call(
        functools.partial(kernel, n_seq, tok, pairs),
        out_shape=jax.ShapeDtypeStruct((tok, half), BF16),
        in_specs=[pl.BlockSpec(memory_space=pl.ANY)] * 4,
        out_specs=pl.BlockSpec(memory_space=pltpu.VMEM),
        scratch_shapes=scratch,
        compiler_params=pltpu.CompilerParams(
            collective_id=0, has_side_effects=True, vmem_limit_bytes=56 * 1024 * 1024),
    )(queries, key_rows, value_rows, out_weight)


def solution(mesh):
    return jax.shard_map(
        functools.partial(local, mesh.shape["seq"]),
        mesh=mesh,
        in_specs=(P("seq", "head"), P("seq", "head"), P("seq", "head"), P("head", None)),
        out_specs=P("seq", "head"),
        check_vma=False,
    )
```

time: 586 us -> 105 us (0.18); the launches traced: 577 us -> 105 us
  local copies, waits for them, and re-layouts: 214 us -> 2.26 us
  starting transfers between devices: 135 us -> 0 us
  Pallas kernels: 0 us -> 103 us
  waiting for transfers between devices: 91.8 us -> 0 us
  other arithmetic: 84.4 us -> 0 us
  matrix products: 36.2 us -> 0 us
  between operations: 14.9 us -> 0.01 us
    ppermute x36 -> x0, starting transfers between devices: 135 us -> none  [the longest x30 116 us: shifted(): lax.ppermute(value, axis, [(source, source + steps) for source in range(l...]
    pallas_call x0 -> x1, Pallas kernels: none -> 103 us  [local(): pl.pallas_call(functools.partial(kernel, n_seq, tok, pairs), out_shape=ja...]
    ppermute x36 -> x0, waiting for transfers between devices: 74.2 us -> none  [the longest x30 74.2 us: shifted(): lax.ppermute(value, axis, [(source, source + steps) for source in range(l...]
    slice x28 -> x0, local copies, waits for them, and re-layouts: 62.5 us -> none  [the longest x10 22.7 us: local_level(): value_blocks[offset:offset + blocks]]
    reshape x35 -> x0, local copies, waits for them, and re-layouts: 57.1 us -> none  [the longest x10 34.1 us: local(): numerator = jnp.repeat(numerator, factor, axis=0)]
    convert_element_type x18 -> x0, other arithmetic: 48.3 us -> none  [the longest x12 23.7 us: coarsen(): ((widened[..., 0, :] + widened[..., 1, :]) * 0.5).astype(jnp.bfloat16)]
    dot_general x15 -> x0, matrix products: 36.2 us -> none  [the longest x7 20.8 us: attend_groups(): jnp.einsum('ghqk,gkhd->gqhd', weights.astype(jnp.bfloat16), value_part, p...]
    unnamed x89 -> x1, local copies, waits for them, and re-layouts: 24.3 us -> 2.26 us
  transfers between devices with their start and end apart: 37 -> 0, of which waited for: 13 -> 0; matrix products, arithmetic and copies ran while one was open for 35% -> 0% of each run, Pallas kernels for 0% -> 0%
where the time goes in v1:
time: 105 us
  Pallas kernels  103 us (98%)
  local copies, waits for them, and re-layouts  2.26 us (2%)
    pallas_call x1, Pallas kernels, local(): pl.pallas_call(functools.partial(kernel, n_seq, tok, pairs), out_shape=ja...  103 us
    unnamed x1, local copies, waits for them, and re-layouts  2.26 us

profile of v1, /device:TPU:29, one launch (start us, length us, event | category | flops | bytes accessed | tf_op | source)
XLA Modules:
  0.0 105.2 jit_solution(3724934786672995224)
XLA Ops:
  0.0 102.9 %shard_map.46 = bf16[1024,512]{1,0:T(8,128)(2,1)} custom-call(bf16[1024,512]{1,0:T(8,128)(2,1)} %q_hbm.1, bf16[1024,512]{1,0:T(8,128)(2,1)} %k_hbm.1, bf16[1024,512]{1,0:T(8,128)(2,1)} %v_hbm.1, bf16[512,1024]{1,0:T(8,128)(2,1)} %w_hbm.1), custom_call_target="tpu_custom_call" | custom-call | tf_op jit(solution)/shard_map/pallas_call | solution.py:330
  103.0 2.3 %copy.6 = bf16[1024,512]{1,0:T(8,128)(2,1)} copy(bf16[1024,512]{1,0:T(8,128)(2,1)} %shard_map.46) | data formatting | bytes 2097152

commit v2 on v1

--- a/solution.py
+++ b/solution.py
@@ -40,13 +40,14 @@
     nums = take(LEVELS)
     tots = take(LEVELS)
     mxs = take(LEVELS)
-    tmp, att, w_s, psend, precv, load_sem, send_sem, recv_sem, psend_sem, precv_sem = scratch
+    tmp, att, w_s, psend, precv, load_sem, send_sem, recv_sem, pair_sem, psend_sem, precv_sem = scratch
 
     me = lax.axis_index("seq")
     head = lax.axis_index("head")
     rows_of = [tok >> l for l in range(LEVELS)]
     span_of = [max(1, BLOCK // r) for r in rows_of]
     half = o_ref.shape[1]
+    first_up = next(l for l in range(LEVELS) if span_of[l] > 1)
 
     loads = []
     for p in range(pairs):
@@ -61,31 +62,27 @@
         c.start()
     w_load.start()
 
-    top = span_of[-1]
-    top_block = me // top
-    top_blocks = n_seq // top
+    exists = []
+    for l in range(LEVELS):
+        n = span_of[l]
+        exists.append((me >= n, me + n < n_seq))
+
     barrier = pltpu.get_barrier_semaphore()
     pl.semaphore_signal(barrier, inc=1, device_id={"head": 1 - head}, device_id_type=MESH)
-    for delta in (-1, 0, 1):
-        there = top_block + delta
-
-        @pl.when((there >= 0) & (there < top_blocks))
-        def _():
-            for j in range(top):
-                other = there * top + j
-
-                @pl.when(other != me)
-                def _():
-                    pl.semaphore_signal(
-                        barrier, inc=1, device_id={"seq": other}, device_id_type=MESH)
-
-    exists = []
+    greeted = 1
+    for n in sorted(set(span_of)):
+        for there in (me - n, me + n):
+            inside = (there >= 0) & (there < n_seq)
+            greeted = greeted + jnp.where(inside, 1, 0)
+
+            @pl.when(inside)
+            def _():
+                pl.semaphore_signal(
+                    barrier, inc=1, device_id={"seq": there}, device_id_type=MESH)
+
     for l in range(LEVELS):
-        block = me // span_of[l]
-        has_left = block >= 1
-        has_right = block + 1 < n_seq // span_of[l]
-        exists.append((has_left, has_right))
-        r = rows_of[l]
+        has_left, has_right = exists[l]
+        r = max(rows_of[l], BLOCK)
 
         @pl.when(jnp.logical_not(has_left))
         def _():
@@ -95,75 +92,96 @@
         def _():
             kv[l][:, :, pl.ds(BLOCK + r, BLOCK), :] = jnp.zeros((2, pairs, BLOCK, LANES), BF16)
 
-    around = jnp.minimum(top_block, 1) + jnp.minimum(top_blocks - 1 - top_block, 1)
-    pl.semaphore_wait(barrier, top + top * around)
-
-    def copies(l, side):
-        r, n = rows_of[l], span_of[l]
-        block, place = me // n, lax.rem(me, n)
-        if r >= BLOCK:
-            length = BLOCK if l == 0 else BLOCK // 2
-            if side == 1:
-                src, dst = BLOCK + r - BLOCK, 0
-            else:
-                src = BLOCK + BLOCK - length
-                dst = BLOCK + r + BLOCK - length
-        else:
-            length = r
-            src = BLOCK
-            dst = place * r + (0 if side == 1 else BLOCK + r)
-            dst = pl.multiple_of(dst, r)
-        out = []
-        for j in range(n):
-            target = (block + (1 if side == 1 else -1)) * n + j
-            out.append(pltpu.make_async_remote_copy(
-                src_ref=kv[l].at[:, :, pl.ds(src, length)],
-                dst_ref=kv[l].at[:, :, pl.ds(dst, length)],
-                send_sem=send_sem.at[l, side, j],
-                recv_sem=recv_sem.at[l, 1 - side],
-                device_id={"seq": target},
-                device_id_type=MESH))
-        return out
+    pl.semaphore_wait(barrier, greeted)
+
+    HALF = BLOCK // 2
+
+    def child(l):
+        return lax.rem(me // span_of[l - 1], 2)
+
+    def plans(l, side):
+        r = max(rows_of[l], BLOCK)
+        far = BLOCK + r
+        if l == 0 or l == first_up:
+            return [(None, BLOCK, r, 0) if side else (None, BLOCK, BLOCK, far)]
+        part = (None, HALF, r, 0) if side else (None, HALF, BLOCK + HALF, far + HALF)
+        if l < first_up:
+            return [part]
+        whole = (None, BLOCK, r, 0) if side else (None, BLOCK, BLOCK, far)
+        c = child(l)
+        whole_if, part_if = (c == 1, c == 0) if side else (c == 0, c == 1)
+        return [(whole_if,) + whole[1:], (part_if,) + part[1:]]
+
+    def each(l, side, act):
+        for cond, length, src, dst in plans(l, side):
+            n = span_of[l]
+            on = exists[l][side] if cond is None else exists[l][side] & cond
+
+            @pl.when(on)
+            def _():
+                act(pltpu.make_async_remote_copy(
+                    src_ref=kv[l].at[:, :, pl.ds(src, length)],
+                    dst_ref=kv[l].at[:, :, pl.ds(dst, length)],
+                    send_sem=send_sem.at[l, side],
+                    recv_sem=recv_sem.at[l, 1 - side],
+                    device_id={"seq": me + n if side else me - n},
+                    device_id_type=MESH))
 
     def start(l):
         for side in (0, 1):
-            @pl.when(exists[l][side])
-            def _():
-                for c in copies(l, side):
-                    c.start()
+            each(l, side, lambda copy: copy.start())
 
     def wait(l):
-        r = rows_of[l]
         for side in (0, 1):
-            length = BLOCK // 2 if (r >= BLOCK and l > 0) else BLOCK
-            if side == 0:
-                at = 0
-            else:
-                at = BLOCK + r + BLOCK - length
-
-            @pl.when(exists[l][side])
-            def _():
-                region = kv[l].at[:, :, pl.ds(at, length)]
-                pltpu.make_async_copy(region, region, recv_sem.at[l, side]).wait()
+            for cond, length, _, dst in plans(l, 1 - side):
+                on = exists[l][side] if cond is None else exists[l][side] & cond
+
+                @pl.when(on)
+                def _():
+                    region = kv[l].at[:, :, pl.ds(dst, length)]
+                    pltpu.make_async_copy(region, region, recv_sem.at[l, side]).wait()
+
+    place = lax.rem(me, 2)
+    part_at = pl.ds(pl.multiple_of(BLOCK + place * HALF, HALF), HALF)
+    pair_copy = pltpu.make_async_remote_copy(
+        src_ref=kv[first_up].at[:, :, part_at],
+        dst_ref=kv[first_up].at[:, :, part_at],
+        send_sem=pair_sem.at[0], recv_sem=pair_sem.at[1],
+        device_id={"seq": me + 1 - 2 * place}, device_id_type=MESH)
+    other_at = pl.ds(pl.multiple_of(BLOCK + (1 - place) * HALF, HALF), HALF)
+
+    def pair_wait():
+        region = kv[first_up].at[:, :, other_at]
+        pltpu.make_async_copy(region, region, pair_sem.at[1]).wait()
 
     for c in loads:
         c.wait()
     start(0)
 
-    for l in range(1, LEVELS):
-        r = rows_of[l]
-        step = min(BLOCK, 2 * r)
-
-        def coarse(p, _, l=l, r=r, step=step):
+    def coarse_keys(p, _):
+        for l in range(1, first_up):
+            for at in range(0, 2 * rows_of[l], BLOCK):
+                for s in range(2):
+                    kv[l][s, p, pl.ds(BLOCK + at // 2, HALF), :] = pool(
+                        kv[l - 1][s, p, pl.ds(BLOCK + at, BLOCK), :])
+        for s in range(2):
+            kv[first_up][s, p, part_at, :] = pool(kv[first_up - 1][s, p, pl.ds(BLOCK, BLOCK), :])
+        return 0
+
+    lax.fori_loop(0, pairs, coarse_keys, 0)
+    pair_copy.start()
+    for l in range(1, first_up):
+        start(l)
+
+    def coarse_queries(p, _):
+        for l in range(1, LEVELS):
+            r = rows_of[l]
+            step = min(BLOCK, 2 * r)
             for at in range(0, 2 * r, step):
-                for s in range(2):
-                    kv[l][s, p, pl.ds(BLOCK + at // 2, step // 2), :] = pool(
-                        kv[l - 1][s, p, pl.ds(BLOCK + at, step), :])
                 qs[l][p, pl.ds(at // 2, step // 2), :] = pool(qs[l - 1][p, pl.ds(at, step), :])
-            return 0
-
-        lax.fori_loop(0, pairs, coarse, 0)
-        start(l)
+        return 0
+
+    lax.fori_loop(0, pairs, coarse_queries, 0)
 
     lane = lax.broadcasted_iota(jnp.int32, (1, LANES), 1)
     low = lane < HEAD_DIM
@@ -181,7 +199,7 @@
         if r >= BLOCK:
             left_at, right_at = j * BLOCK, (j + 2) * BLOCK
         else:
-            left_at, right_at = 0, BLOCK + r
+            left_at, right_at = 0, 2 * BLOCK
         left_bias = bias_of(has_left) if j == 0 else None
         right_bias = bias_of(has_right) if j == blocks - 1 else None
         if l == 0:
@@ -235,20 +253,57 @@
 
         lax.fori_loop(0, pairs, body, 0)
 
-    blocks0 = max(1, tok // BLOCK)
+    def gather(l):
+        c = child(l)
+        own = pl.ds(pl.multiple_of(BLOCK + c * HALF, HALF), HALF)
+        sibling = pl.ds(pl.multiple_of(BLOCK + (1 - c) * HALF, HALF), HALF)
+        sibling_from = pl.ds(pl.multiple_of((1 - c) * 2 * BLOCK, BLOCK), BLOCK)
+        beside = pl.ds(pl.multiple_of(HALF + c * 3 * HALF, HALF), HALF)
+        beside_from = pl.ds(pl.multiple_of(c * 2 * BLOCK, BLOCK), BLOCK)
+
+        def body(p, _):
+            for s in range(2):
+                below = kv[l - 1]
+                kv[l][s, p, own, :] = pool(below[s, p, pl.ds(BLOCK, BLOCK), :])
+                kv[l][s, p, sibling, :] = pool(below[s, p, sibling_from, :])
+                kv[l][s, p, beside, :] = pool(below[s, p, beside_from, :])
+            return 0
+
+        lax.fori_loop(0, pairs, body, 0)
+
+    blocks0 = tok // BLOCK
     inner = list(range(1, blocks0 - 1))
     outer = [j for j in range(blocks0) if j not in inner]
-    for j in inner:
+    pieces = inner[:1], inner[1:], outer[:1], outer[1:]
+    for j in pieces[0]:
+        phase(0, [j])
+    pair_wait()
+    start(first_up)
+    for j in pieces[1]:
         phase(0, [j])
     wait(0)
-    for j in outer:
+    for j in pieces[2]:
         phase(0, [j])
-    for l in range(1, LEVELS):
+    ups = list(range(first_up, LEVELS))
+    wait(first_up)
+    if len(ups) > 1:
+        gather(ups[1])
+        start(ups[1])
+    for j in pieces[3]:
+        phase(0, [j])
+    for l in range(1, first_up):
         wait(l)
-        if rows_of[l] >= BLOCK:
-            near(l)
-        for j in range(max(1, rows_of[l] // BLOCK)):
+        near(l)
+        for j in range(rows_of[l] // BLOCK):
             phase(l, [j])
+        if l + 1 < len(ups):
+            wait(ups[l])
+            gather(ups[l + 1])
+            start(ups[l + 1])
+    for l in ups[:-1]:
+        phase(l, [0])
+    wait(ups[-1])
+    phase(ups[-1], [0])
 
     def join(p, _):
         cur = (nums[-1][p], tots[-1][p], mxs[-1][p])
@@ -293,12 +348,10 @@
         o_ref[at, :] = (own.astype(F32) + precv[at, :].astype(F32)).astype(BF16)
     for c in range(chunks):
         part_copy(c).wait_send()
+    pair_copy.wait_send()
     for l in range(LEVELS):
         for side in (0, 1):
-            @pl.when(exists[l][side])
-            def _():
-                for c in copies(l, side):
-                    c.wait_send()
+            each(l, side, lambda copy: copy.wait_send())
 
 
 def local(n_seq, queries, key_rows, value_rows, out_weight):
@@ -307,11 +360,11 @@
     width = out_weight.shape[1]
     half = width // 2
     rows_of = [tok >> l for l in range(LEVELS)]
-    top = max(1, BLOCK // rows_of[-1])
+    assert rows_of[0] % BLOCK == 0 and BLOCK in rows_of
     chunks = tok // min(BLOCK, tok)
     results = [pltpu.VMEM((pairs, r, LANES), F32) for r in rows_of]
     scratch = (
-        [pltpu.VMEM((2, pairs, r + 2 * BLOCK, LANES), BF16) for r in rows_of]
+        [pltpu.VMEM((2, pairs, max(r, BLOCK) + 2 * BLOCK, LANES), BF16) for r in rows_of]
         + [pltpu.VMEM((pairs, r, LANES), BF16) for r in rows_of]
         + results * 3
         + [
@@ -321,8 +374,9 @@
             pltpu.VMEM((tok, half), BF16),
             pltpu.VMEM((tok, half), BF16),
             pltpu.SemaphoreType.DMA((4, pairs)),
-            pltpu.SemaphoreType.DMA((LEVELS, 2, top)),
             pltpu.SemaphoreType.DMA((LEVELS, 2)),
+            pltpu.SemaphoreType.DMA((LEVELS, 2)),
+            pltpu.SemaphoreType.DMA((2,)),
             pltpu.SemaphoreType.DMA((chunks,)),
             pltpu.SemaphoreType.DMA((chunks,)),
         ]

time: 105 us -> 118 us (1.12)
  the two profiles are of different devices: /device:TPU:29 before, /device:TPU:0 now
where the time goes in v2:
time: 118 us; the launch traced here: 117 us
  Pallas kernels  115 us (97%)
  local copies, waits for them, and re-layouts  2.26 us (2%)
    pallas_call x1, Pallas kernels, local(): pl.pallas_call(functools.partial(kernel, n_seq, tok, pairs), out_shape=ja...  115 us

profile of v2, /device:TPU:0, one launch (start us, length us, event | category | flops | bytes accessed | tf_op | source)
XLA Modules:
  0.0 117.4 jit_solution(7997762651704841746)
XLA Ops:
  0.0 115.2 %shard_map.46 = bf16[1024,512]{1,0:T(8,128)(2,1)} custom-call(bf16[1024,512]{1,0:T(8,128)(2,1)} %q_hbm.1, bf16[1024,512]{1,0:T(8,128)(2,1)} %k_hbm.1, bf16[1024,512]{1,0:T(8,128)(2,1)} %v_hbm.1, bf16[512,1024]{1,0:T(8,128)(2,1)} %w_hbm.1), custom_call_target="tpu_custom_call" | custom-call | tf_op jit(solution)/shard_map/pallas_call | solution.py:384
  115.2 2.3 %copy.6 = bf16[1024,512]{1,0:T(8,128)(2,1)} copy(bf16[1024,512]{1,0:T(8,128)(2,1)} %shard_map.46) | data formatting | bytes 2097152

commit v3 on v1

--- a/solution.py
+++ b/solution.py
@@ -19,12 +19,17 @@
 F32 = jnp.float32
 
 
-def pool(x):
-    rows = x.shape[0]
-    r = lax.broadcasted_iota(jnp.int32, (rows // 2, rows), 0)
-    c = lax.broadcasted_iota(jnp.int32, (rows // 2, rows), 1)
-    mat = jnp.where((c == 2 * r) | (c == 2 * r + 1), 0.5, 0.0).astype(BF16)
-    return jnp.dot(mat, x, preferred_element_type=F32).astype(BF16)
+def pool_matrix():
+    r = lax.broadcasted_iota(jnp.int32, (BLOCK // 2, BLOCK), 0)
+    c = lax.broadcasted_iota(jnp.int32, (BLOCK // 2, BLOCK), 1)
+    return jnp.where((c == 2 * r) | (c == 2 * r + 1), 0.5, 0.0).astype(BF16)
+
+
+def pooled(mat_ref, parts):
+    rows = parts[0].shape[0]
+    mat = mat_ref[pl.ds(0, rows // 2), pl.ds(0, rows)]
+    out = jnp.dot(mat, jnp.concatenate(parts, axis=1), preferred_element_type=F32).astype(BF16)
+    return [out[:, i * LANES:(i + 1) * LANES] for i in range(len(parts))]
 
 
 def kernel(n_seq, tok, pairs, q_hbm, k_hbm, v_hbm, w_hbm, o_ref, *scratch):
@@ -40,7 +45,7 @@
     nums = take(LEVELS)
     tots = take(LEVELS)
     mxs = take(LEVELS)
-    tmp, att, w_s, psend, precv, load_sem, send_sem, recv_sem, psend_sem, precv_sem = scratch
+    mat, tmp, att, w_s, psend, precv, load_sem, send_sem, recv_sem, psend_sem, precv_sem = scratch
 
     me = lax.axis_index("seq")
     head = lax.axis_index("head")
@@ -60,6 +65,7 @@
     for c in loads:
         c.start()
     w_load.start()
+    mat[...] = pool_matrix()
 
     top = span_of[-1]
     top_block = me // top
@@ -154,15 +160,16 @@
         r = rows_of[l]
         step = min(BLOCK, 2 * r)
 
-        def coarse(p, _, l=l, r=r, step=step):
+        for p in range(pairs):
             for at in range(0, 2 * r, step):
-                for s in range(2):
-                    kv[l][s, p, pl.ds(BLOCK + at // 2, step // 2), :] = pool(
-                        kv[l - 1][s, p, pl.ds(BLOCK + at, step), :])
-                qs[l][p, pl.ds(at // 2, step // 2), :] = pool(qs[l - 1][p, pl.ds(at, step), :])
-            return 0
-
-        lax.fori_loop(0, pairs, coarse, 0)
+                to = pl.ds(BLOCK + at // 2, step // 2)
+                k, v, q = pooled(mat, [
+                    kv[l - 1][0, p, pl.ds(BLOCK + at, step), :],
+                    kv[l - 1][1, p, pl.ds(BLOCK + at, step), :],
+                    qs[l - 1][p, pl.ds(at, step), :]])
+                kv[l][0, p, to, :] = k
+                kv[l][1, p, to, :] = v
+                qs[l][p, pl.ds(at // 2, step // 2), :] = q
         start(l)
 
     lane = lax.broadcasted_iota(jnp.int32, (1, LANES), 1)
@@ -173,7 +180,7 @@
     def bias_of(valid):
         return jnp.where(valid, 0.0, NEG_LARGE).astype(F32)
 
-    def attend(l, j, p):
+    def scores(l, j, p):
         r = rows_of[l]
         size = min(BLOCK, r)
         has_left, has_right = exists[l]
@@ -191,7 +198,7 @@
         q = qs[l][p, pl.ds(j * BLOCK, size), :]
         ks = [kv[l][0, p, pl.ds(at, BLOCK), :] for at, _ in segments]
         vs = [kv[l][1, p, pl.ds(at, BLOCK), :] for at, _ in segments]
-        accs, peaks = [], []
+        sums, v_es = [], []
         for e in (0, 1):
             mine = masks[e]
             other = masks[1 - e]
@@ -203,21 +210,31 @@
                     k = k + (other.astype(F32) * bias).astype(BF16)
                 k_e.append(k)
             k_e = jnp.concatenate(k_e, axis=0)
-            v_e = jnp.concatenate([v * mine + other for v in vs], axis=0)
-            s = lax.dot_general(q_e, k_e, (((1,), (1,)), ((), ())), preferred_element_type=F32)
+            v_es.append(jnp.concatenate([v * mine + other for v in vs], axis=0))
+            sums.append(lax.dot_general(
+                q_e, k_e, (((1,), (1,)), ((), ())), preferred_element_type=F32))
+        return sums, v_es
+
+    def finish(l, j, p, sums, v_es):
+        accs, peaks = [], []
+        for s, v_e in zip(sums, v_es):
             peak = jnp.max(s, axis=1, keepdims=True)
             weights = jnp.exp(s - peak).astype(BF16)
             accs.append(jnp.dot(weights, v_e, preferred_element_type=F32))
             peaks.append(peak)
-        at = pl.ds(j * BLOCK, size)
+        at = pl.ds(j * BLOCK, min(BLOCK, rows_of[l]))
         nums[l][p, at, :] = jnp.where(low, accs[0], accs[1])
         tots[l][p, at, :] = pltpu.roll(jnp.where(low, accs[1], accs[0]), HEAD_DIM, 1)
         mxs[l][p, at, :] = jnp.where(low, peaks[0], peaks[1]) + l * LOG_TWO
 
-    def phase(l, which):
+    def phase(which):
         def body(p, _):
-            for j in which:
-                attend(l, j, p)
+            ahead = scores(*which[0], p)
+            for i, (l, j) in enumerate(which):
+                now = ahead
+                if i + 1 < len(which):
+                    ahead = scores(*which[i + 1], p)
+                finish(l, j, p, *now)
             return 0
 
         lax.fori_loop(0, pairs, body, 0)
@@ -225,30 +242,32 @@
     def near(l):
         r, below = rows_of[l], rows_of[l - 1]
 
-        def body(p, _):
-            for s in range(2):
-                kv[l][s, p, pl.ds(BLOCK // 2, BLOCK // 2), :] = pool(
-                    kv[l - 1][s, p, pl.ds(0, BLOCK), :])
-                kv[l][s, p, pl.ds(BLOCK + r, BLOCK // 2), :] = pool(
-                    kv[l - 1][s, p, pl.ds(BLOCK + below, BLOCK), :])
-            return 0
-
-        lax.fori_loop(0, pairs, body, 0)
+        for p in range(pairs):
+            k, v = pooled(mat, [kv[l - 1][s, p, pl.ds(0, BLOCK), :] for s in range(2)])
+            kv[l][0, p, pl.ds(BLOCK // 2, BLOCK // 2), :] = k
+            kv[l][1, p, pl.ds(BLOCK // 2, BLOCK // 2), :] = v
+            k, v = pooled(
+                mat, [kv[l - 1][s, p, pl.ds(BLOCK + below, BLOCK), :] for s in range(2)])
+            kv[l][0, p, pl.ds(BLOCK + r, BLOCK // 2), :] = k
+            kv[l][1, p, pl.ds(BLOCK + r, BLOCK // 2), :] = v
 
     blocks0 = max(1, tok // BLOCK)
     inner = list(range(1, blocks0 - 1))
     outer = [j for j in range(blocks0) if j not in inner]
-    for j in inner:
-        phase(0, [j])
+    if inner:
+        phase([(0, j) for j in inner])
     wait(0)
-    for j in outer:
-        phase(0, [j])
+    phase([(0, j) for j in outer])
+    small = []
     for l in range(1, LEVELS):
         wait(l)
         if rows_of[l] >= BLOCK:
             near(l)
-        for j in range(max(1, rows_of[l] // BLOCK)):
-            phase(l, [j])
+        if rows_of[l] > BLOCK:
+            phase([(l, j) for j in range(rows_of[l] // BLOCK)])
+        else:
+            small.append((l, 0))
+    phase(small)
 
     def join(p, _):
         cur = (nums[-1][p], tots[-1][p], mxs[-1][p])
@@ -315,6 +334,7 @@
         + [pltpu.VMEM((pairs, r, LANES), BF16) for r in rows_of]
         + results * 3
         + [
+            pltpu.VMEM((BLOCK // 2, BLOCK), BF16),
             pltpu.VMEM((3, tok, LANES), F32),
             pltpu.VMEM((tok, columns), BF16),
             pltpu.VMEM(out_weight.shape, BF16),

time: 105 us -> 107 us (1.019)
  Pallas kernels: 103 us -> 105 us
    pallas_call x1, Pallas kernels: 103 us -> 105 us  [local(): pl.pallas_call(functools.partial(kernel, n_seq, tok, pairs), out_shape=ja...]
where the time goes in v3:
time: 107 us
  Pallas kernels  105 us (98%)
  local copies, waits for them, and re-layouts  2.26 us (2%)
    pallas_call x1, Pallas kernels, local(): pl.pallas_call(functools.partial(kernel, n_seq, tok, pairs), out_shape=ja...  105 us
    unnamed x1, local copies, waits for them, and re-layouts  2.26 us

profile of v3, /device:TPU:29, one launch (start us, length us, event | category | flops | bytes accessed | tf_op | source)
XLA Modules:
  0.0 107.3 jit_solution(11764264710271705385)
XLA Ops:
  0.0 105.1 %shard_map.46 = bf16[1024,512]{1,0:T(8,128)(2,1)} custom-call(bf16[1024,512]{1,0:T(8,128)(2,1)} %q_hbm.1, bf16[1024,512]{1,0:T(8,128)(2,1)} %k_hbm.1, bf16[1024,512]{1,0:T(8,128)(2,1)} %v_hbm.1, bf16[512,1024]{1,0:T(8,128)(2,1)} %w_hbm.1), custom_call_target="tpu_custom_call" | custom-call | tf_op jit(solution)/shard_map/pallas_call | solution.py:350
  105.1 2.3 %copy.6 = bf16[1024,512]{1,0:T(8,128)(2,1)} copy(bf16[1024,512]{1,0:T(8,128)(2,1)} %shard_map.46) | data formatting | bytes 2097152
